TPU v7x, 128 devices: a whole 4x4x4 slice. The times are simulated.
128 devices in a mesh: row: 8 (over x, core), col: 16 (over y, z).
Axes of the slice: x: 4, y: 4, z: 4, core: 2. Of those that a mesh axis runs over, the one named last changes fastest.
Arguments:
- nodes: bfloat16 [8192, 512], P(('row', 'col')), may hold values from -6 to 6
- edges: bfloat16 [8, 16, 4096, 512], P('row', 'col'), may hold values from -6 to 6
- senders: int32 [8, 16, 4096], P('row', 'col'), may hold values from 0 to 511
- receivers: int32 [8, 16, 4096], P('row', 'col'), may hold values from 0 to 1023
- levels: int32 [8, 16, 4096], P('row', 'col'), may hold values from 0 to 6
- counts: int32 [8, 16], P('row', 'col'), may hold values from 1 to 4096, as said below
- edge_w1: bfloat16 [3, 512, 512], replicated, may hold values from -0.15625 to 0.15625
- level_bias: bfloat16 [7, 512], replicated, may hold values from -6 to 6
- edge_w2: bfloat16 [512, 512], replicated, may hold values from -0.25 to 0.25
- edge_gain: float32 [512], replicated, may hold values from 0.1 to 1.9
- node_w1: bfloat16 [2, 512, 512], replicated, may hold values from -0.1875 to 0.1875
- node_w2: bfloat16 [512, 512], replicated, may hold values from -0.25 to 0.25
- node_gain: float32 [512], replicated, may hold values from 0.1 to 1.9
- grid: bfloat16 [131072, 512], P(('row', 'col')), may hold values from -6 to 6
- send_rows: int32 [128, 128, 4], P(('row', 'col')), may hold values from 0 to 63, as said below
- dec_index: int32 [131072, 3], P(('row', 'col')), may hold values from 0 to 511, as said below
- dec_w1: bfloat16 [2, 512, 512], replicated, may hold values from -0.1875 to 0.1875
- dec_w2: bfloat16 [512, 512], replicated, may hold values from -0.25 to 0.25
- dec_gain: float32 [512], replicated, may hold values from 0.1 to 1.9
Outputs:
- nodes_out: bfloat16 [8192, 512], P(('row', 'col'))
- edges_out: bfloat16 [8, 16, 4096, 512], P('row', 'col')
- grid_out: bfloat16 [131072, 512], P(('row', 'col'))
Inputs may be any that keep to these rules, and one draw needn't show every extreme that they name: `senders`: at slots at or beyond the tile's count the index is arbitrary and unused. `receivers`: at slots at or beyond the tile's count the index is arbitrary and unused. `counts`: some tile is full in every draw. `send_rows`: the 4 rows that one device sends to one band device are distinct. `dec_index`: buffer rows are laid out by source device, then slot; every row of a band's buffer is named by some decoder edge of that band.
All inputs are finite; a program needn't handle non-finite values.
Results may differ from a plain program's by a relative error of at most 0.015.
Values may be sent and summed in bfloat16 or wider, within the bound.
No kernel may reach another device: no remote copies, remote signals or barrier semaphores. Data moves between devices by JAX's collectives and lax.ppermute only.
A program may use at most 128 MiB of HBM per device.

v0:
```python
import math
import jax
import jax.numpy as jnp
from jax import lax
from jax.sharding import PartitionSpec as P

EPSILON = 1e-05


def layer_norm(values, gain):
    center = values - jnp.mean(values, axis=-1, keepdims=True)
    spread = jnp.mean(center * center, axis=-1, keepdims=True)
    return center * lax.rsqrt(spread + EPSILON) * gain


def mlp_tail(pre, second_weight, gain):
    hidden = jax.nn.silu(pre).astype(jnp.bfloat16)
    output = jnp.dot(hidden, second_weight, preferred_element_type=jnp.float32)
    return layer_norm(output, gain)


def one_hot_rows(ids, count):
    return (ids[:, None] == jnp.arange(count, dtype=jnp.int32)[None, :]).astype(jnp.bfloat16)


def select_low(table_hot, table):
    return jnp.dot(table_hot, table, preferred_element_type=jnp.float32).astype(jnp.bfloat16)


def on_device(
    nodes,
    edges,
    senders,
    receivers,
    levels,
    counts,
    edge_w1,
    level_bias,
    edge_w2,
    edge_gain,
    node_w1,
    node_w2,
    node_gain,
    grid,
    send_rows,
    dec_index,
    dec_w1,
    dec_w2,
    dec_gain,
):
    node_block = nodes.shape[0]
    width = nodes.shape[1]
    capacity = edges.shape[2]
    level_count = level_bias.shape[0]
    sender_count = node_block * lax.axis_size("row")
    receiver_count = node_block * lax.axis_size("col")
    sender_block = lax.all_gather(nodes, "row", axis=0, tiled=True)
    receiver_block = lax.all_gather(nodes, "col", axis=0, tiled=True)
    joined_weight = edge_w1.reshape(3 * width, width)

    def first_layer(rows, send_hot, recv_hot):
        joined = jnp.concatenate(
            [rows, select_low(send_hot, sender_block), select_low(recv_hot, receiver_block)], axis=1
        )
        return jnp.dot(joined, joined_weight, preferred_element_type=jnp.float32)

    block_rows = math.gcd(capacity, 1024)
    block_count = capacity // block_rows
    slot_used = jnp.arange(capacity, dtype=jnp.int32) < counts[0, 0]
    items = (
        edges[0, 0].reshape(block_count, block_rows, width),
        senders[0, 0].reshape(block_count, block_rows),
        receivers[0, 0].reshape(block_count, block_rows),
        levels[0, 0].reshape(block_count, block_rows),
        slot_used.reshape(block_count, block_rows),
    )

    def edge_block(partial_value, item):
        rows, send_ids, recv_ids, level_ids, used = item
        send_hot = one_hot_rows(send_ids, sender_count)
        recv_hot = one_hot_rows(recv_ids, receiver_count)
        pre = first_layer(rows, send_hot, recv_hot)
        pre = pre + jnp.dot(
            one_hot_rows(level_ids, level_count), level_bias, preferred_element_type=jnp.float32
        )
        message = mlp_tail(pre, edge_w2, edge_gain).astype(jnp.bfloat16)
        kept = jnp.where(used[:, None], message, jnp.zeros((), jnp.bfloat16))
        updated = (rows.astype(jnp.float32) + kept.astype(jnp.float32)).astype(jnp.bfloat16)
        partial_value = partial_value + lax.dot_general(
            recv_hot, kept, (((0,), (0,)), ((), ())), preferred_element_type=jnp.float32
        )
        return (partial_value, updated)

    partial_value, edge_new = lax.scan(
        edge_block, jnp.zeros((receiver_count, width), jnp.float32), items
    )
    edges_out = edge_new.reshape(1, 1, capacity, width)
    summed = lax.psum(partial_value.astype(jnp.bfloat16), "col").astype(jnp.float32)
    aggregated = lax.dynamic_slice_in_dim(summed, lax.axis_index("col") * node_block, node_block, 0)
    node_pre = jnp.dot(nodes, node_w1[0], preferred_element_type=jnp.float32)
    node_pre = node_pre + jnp.dot(
        aggregated.astype(jnp.bfloat16), node_w1[1], preferred_element_type=jnp.float32
    )
    nodes_out = (nodes.astype(jnp.float32) + mlp_tail(node_pre, node_w2, node_gain)).astype(
        jnp.bfloat16
    )
    peers = send_rows.shape[1]
    per_peer = send_rows.shape[2]
    picked = select_low(one_hot_rows(send_rows[0].reshape(-1), node_block), nodes_out).reshape(
        peers, per_peer, width
    )
    received = lax.all_to_all(picked, ("row", "col"), split_axis=0, concat_axis=0, tiled=True)
    cells = grid.shape[0]
    fan_count = dec_index.shape[1]
    chosen = select_low(
        one_hot_rows(dec_index.reshape(-1), peers * per_peer),
        received.reshape(peers * per_peer, width),
    )
    node_dec = jnp.dot(chosen, dec_w1[1], preferred_element_type=jnp.float32).reshape(
        cells, fan_count, width
    )
    grid_part = jnp.dot(grid, dec_w1[0], preferred_element_type=jnp.float32)
    dec_pre = grid_part[:, None, :] + node_dec
    messages = mlp_tail(dec_pre.reshape(cells * fan_count, width), dec_w2, dec_gain).reshape(
        cells, fan_count, width
    )
    grid_out = (grid.astype(jnp.float32) + jnp.sum(messages, axis=1)).astype(jnp.bfloat16)
    return (nodes_out, edges_out, grid_out)


def solution(mesh):
    return jax.shard_map(
        on_device,
        mesh=mesh,
        in_specs=(
            P(("row", "col"), None),
            P("row", "col", None, None),
            P("row", "col", None),
            P("row", "col", None),
            P("row", "col", None),
            P("row", "col"),
            P(),
            P(),
            P(),
            P(),
            P(),
            P(),
            P(),
            P(("row", "col"), None),
            P(("row", "col"), None, None),
            P(("row", "col"), None),
            P(),
            P(),
            P(),
        ),
        out_specs=(P(("row", "col"), None), P("row", "col", None, None), P(("row", "col"), None)),
        check_vma=False,
    )
```

profile of v0, /device:TPU:1, one launch (start us, length us, event | category | flops | bytes accessed | tf_op | source)
XLA Modules:
  0.0 344.8 jit_solution(2025392052135723121)
XLA Ops:
  13.4 15.0 %all_gather.6 = bf16[512,512]{1,0:T(8,128)(2,1)S(1)} all-gather(bf16[64,512]{1,0:T(8,128)(2,1)} %param.21), channel_id=1, replica_groups=mesh['row'=8,'col'=16] {'row'}, dimensions={0}, use_global_device_ids=true | all-gather | bytes 589824 | tf_op jit(solution)/shard_map/all_gather | solution.py:57
  28.4 26.4 %all-gather.2.cloned.1.call-done = bf16[1024,512]{1,0:T(8,128)(2,1)} async-done(((bf16[64,512]{1,0:T(8,128)(2,1)}), bf16[1024,512]{1,0:T(8,128)(2,1)}) %all-gather.2.cloned.1.call-update) | async-done | bytes 1048592 | tf_op jit(solution)/shard_map/all_gather | solution.py:58
  54.8 99.2 %while.13 = (s32[]{:T(128)}, f32[1024,512]{1,0:T(8,128)}, bf16[4,1024,512]{2,1,0:T(8,128)(2,1)}, s32[4,1024]{1,0:T(4,128)S(1)}, pred[4,1024]{1,0:T(4,128)(4,1)S(...) while((s32[]{:T(128)}, f32[1024,512]{1,0:T(8,128)}, ...), condition=%wide.region_3.4_spmd.clone, body=%wide.region_0.3_spmd.clone.sunk | while | flops 4866973696 | bytes 48897348 | solution.py:94
  62.1 5.2 %fusion.97 = f32[1024,512]{1,0:T(8,128)} fusion(bf16[1536,512]{1,0:T(8,128)(2,1)} %get-tuple-element.307, bf16[1024,512]{0,1:T(8,128)(2,1)} %fusion.95, bf16[1024,512]{0,1:T(8,128)(2,1)} %fusion.96, bf16[1024,512]{0,1:T(8,128)(2,1)S(1)} %bitcast.64), kind=kOutput, calls=%fused_computation.3.clone.1 | convolution fusion | flops 1620049920 | bytes 6815744 | tf_op jit(solution)/shard_map/while/body/eval_jaxpr/dot_general | solution.py:65
  72.9 3.0 select_add_fusion.2
  85.7 5.2 %fusion.97 = f32[1024,512]{1,0:T(8,128)} fusion(bf16[1536,512]{1,0:T(8,128)(2,1)} %get-tuple-element.307, bf16[1024,512]{0,1:T(8,128)(2,1)} %fusion.95, bf16[1024,512]{0,1:T(8,128)(2,1)} %fusion.96, bf16[1024,512]{0,1:T(8,128)(2,1)S(1)} %bitcast.64), kind=kOutput, calls=%fused_computation.3.clone.1 | convolution fusion | flops 1620049920 | bytes 6815744 | tf_op jit(solution)/shard_map/while/body/eval_jaxpr/dot_general | solution.py:65
  90.9 2.9 fusion.98
  96.5 4.6 %select_add_fusion.2 = f32[1024,512]{1,0:T(8,128)} fusion(f32[1024,512]{1,0:T(8,128)} %get-tuple-element.283, s32[1024]{0:T(1024)S(1)} %bitcast.67, pred[]{:T(512)S(6)} %compare.3, f32[1024,512]{0,1:T(8,128)S(1)} %get-tuple-element.264, f32[512]{0:T(512)S(1)} %copy-done.6, f32[1024]{0:T(1024)S(1)} %add_rsqrt_fusion.4, ...), kind=kOutput, calls=%fused_computation.10.clone.1 | convolution fusion | flops 1079508992 | bytes 6306817 | tf_op jit(solution)/shard_map/while/body/eval_jaxpr/dot_general | solution.py:89
  110.9 5.2 %fusion.97 = f32[1024,512]{1,0:T(8,128)} fusion(bf16[1536,512]{1,0:T(8,128)(2,1)} %get-tuple-element.307, bf16[1024,512]{0,1:T(8,128)(2,1)} %fusion.95, bf16[1024,512]{0,1:T(8,128)(2,1)} %fusion.96, bf16[1024,512]{0,1:T(8,128)(2,1)S(1)} %bitcast.64), kind=kOutput, calls=%fused_computation.3.clone.1 | convolution fusion | flops 1620049920 | bytes 6815744 | tf_op jit(solution)/shard_map/while/body/eval_jaxpr/dot_general | solution.py:65
  121.7 4.5 %select_add_fusion.2 = f32[1024,512]{1,0:T(8,128)} fusion(f32[1024,512]{1,0:T(8,128)} %get-tuple-element.283, s32[1024]{0:T(1024)S(1)} %bitcast.67, pred[]{:T(512)S(6)} %compare.3, f32[1024,512]{0,1:T(8,128)S(1)} %get-tuple-element.264, f32[512]{0:T(512)S(1)} %copy-done.6, f32[1024]{0:T(1024)S(1)} %add_rsqrt_fusion.4, ...), kind=kOutput, calls=%fused_computation.10.clone.1 | convolution fusion | flops 1079508992 | bytes 6306817 | tf_op jit(solution)/shard_map/while/body/eval_jaxpr/dot_general | solution.py:89
  136.1 5.2 %fusion.97 = f32[1024,512]{1,0:T(8,128)} fusion(bf16[1536,512]{1,0:T(8,128)(2,1)} %get-tuple-element.307, bf16[1024,512]{0,1:T(8,128)(2,1)} %fusion.95, bf16[1024,512]{0,1:T(8,128)(2,1)} %fusion.96, bf16[1024,512]{0,1:T(8,128)(2,1)S(1)} %bitcast.64), kind=kOutput, calls=%fused_computation.3.clone.1 | convolution fusion | flops 1620049920 | bytes 6815744 | tf_op jit(solution)/shard_map/while/body/eval_jaxpr/dot_general | solution.py:65
  146.9 4.6 %select_add_fusion.2 = f32[1024,512]{1,0:T(8,128)} fusion(f32[1024,512]{1,0:T(8,128)} %get-tuple-element.283, s32[1024]{0:T(1024)S(1)} %bitcast.67, pred[]{:T(512)S(6)} %compare.3, f32[1024,512]{0,1:T(8,128)S(1)} %get-tuple-element.264, f32[512]{0:T(512)S(1)} %copy-done.6, f32[1024]{0:T(1024)S(1)} %add_rsqrt_fusion.4, ...), kind=kOutput, calls=%fused_computation.10.clone.1 | convolution fusion | flops 1079508992 | bytes 6306817 | tf_op jit(solution)/shard_map/while/body/eval_jaxpr/dot_general | solution.py:89
  157.4 86.1 %all-reduce.2.cloned.1.call-done = bf16[1024,512]{1,0:T(8,128)(2,1)} async-done(((bf16[1024,512]{1,0:T(8,128)(2,1)}), bf16[1024,512]{1,0:T(8,128)(2,1)}) %all-reduce.2.cloned.1.call-update) | async-done | bytes 1048592 | tf_op jit(solution)/shard_map/psum | solution.py:98
  246.4 8.8 %all-to-all-start = ((bf16[128,4,512]{2,1,0:T(4,128)(2,1)}), bf16[128,4,512]{2,1,0:T(4,128)(2,1)S(1)}, u32[]{:S(2)}, u32[]{:S(2)}) async-start(bf16[128,4,512]{2,1,0:T(4,128)(2,1)} %reshape.80), calls=%async_computation | async-start | bytes 1048576 | tf_op jit(solution)/shard_map/all_to_all | solution.py:112
  257.8 11.3 %all-to-all-done = bf16[128,4,512]{2,1,0:T(4,128)(2,1)S(1)} async-done(((bf16[128,4,512]{2,1,0:T(4,128)(2,1)}), bf16[128,4,512]{2,1,0:T(4,128)(2,1)S(1)}, u32[]{:S(2)}, u32[]{:S(2)}) %all-to-all-start) | async-done | bytes 524320 | tf_op jit(solution)/shard_map/all_to_all | solution.py:112
  270.0 4.7 %fusion.28 = bf16[3072,512]{1,0:T(8,128)(2,1)} fusion(bf16[512,512]{1,0:T(8,128)(2,1)} %reshape.81, s32[3072]{0:T(1024)S(1)} %eq.75), kind=kOutput, calls=%fused_computation.43 | convolution fusion | flops 1613758464 | bytes 3682304 | tf_op jit(solution)/shard_map/dot_general | solution.py:27
  274.7 9.1 %dot_general.50 = bf16[1024,3,512]{2,1,0:T(4,128)(2,1)} reshape(bf16[3072,512]{1,0:T(8,128)(2,1)} %fusion.28) | data formatting | bytes 6291456 | tf_op jit(solution)/shard_map/dot_general | solution.py:119
  283.8 4.4 %broadcast_add_fusion = f32[1024,3,512]{2,0,1:T(8,128)S(1)} fusion(f32[1024,512]{1,0:T(8,128)S(1)} %fusion.36, bf16[1024,3,512]{2,1,0:T(4,128)(2,1)} %dot_general.50, bf16[2,512,512]{2,1,0:T(8,128)(2,1)} %param.37), kind=kOutput, calls=%fused_computation.47 | convolution fusion | flops 1612185600 | bytes 13107200 | tf_op jit(solution)/shard_map/dot_general | solution.py:119
  288.2 7.5 %copy.29 = f32[1024,3,512]{2,1,0:T(4,128)} copy(f32[1024,3,512]{2,0,1:T(8,128)S(1)} %broadcast_add_fusion) | data formatting | bytes 12582912 | tf_op jit(solution)/shard_map/add | solution.py:123
  295.8 10.8 %reshape.82 = f32[3072,512]{1,0:T(8,128)} reshape(f32[1024,3,512]{2,1,0:T(4,128)} %copy.29) | data formatting | bytes 12582912 | tf_op jit(solution)/shard_map/reshape | solution.py:124
  306.5 4.1 %fusion.62 = (f32[3072]{0:T(1024)S(1)}, f32[3072,512]{1,0:T(8,128)S(1)}) fusion(bf16[512,512]{1,0:T(8,128)(2,1)S(1)} %copy-done, f32[3072,512]{1,0:T(8,128)} %reshape.82), kind=kOutput, calls=%fused_computation.81 | convolution fusion | flops 1620046848 | bytes 13119488 | tf_op jit(solution)/shard_map/dot_general | solution.py:18
  312.7 3.8 %multiply_multiply_fusion = f32[3072,512]{1,0:T(8,128)} fusion(f32[3072,512]{1,0:T(8,128)S(1)} %get-tuple-element.172, f32[512]{0:T(512)S(1)} %copy-done.9, f32[3072]{0:T(1024)S(1)} %add_rsqrt_fusion.1, f32[3072]{0:T(1024)S(1)} %broadcast_multiply_fusion.1), kind=kLoop, calls=%fused_computation.38 | loop fusion | flops 4718592 | bytes 12609536 | tf_op jit(solution)/shard_map/mul | solution.py:13
  316.5 10.5 %reshape.83 = f32[1024,3,512]{2,1,0:T(4,128)} reshape(f32[3072,512]{1,0:T(8,128)} %multiply_multiply_fusion) | data formatting | bytes 12582912 | tf_op jit(solution)/shard_map/reshape | solution.py:124
  327.0 8.4 %reduce_sum.67 = f32[1024,512]{1,0:T(8,128)S(1)} reduce(f32[1024,3,512]{2,1,0:T(4,128)} %reshape.83, f32[]{:T(128)} %constant.51.clone.1), dimensions={1}, to_apply=%region_9.10 | reduce | flops 1048576 | bytes 8388612 | tf_op jit(solution)/shard_map/reduce_sum | solution.py:127
  (146 shorter events, 78.4 us)
Async XLA Ops:
  7.2 299.4 %copy-start = (bf16[512,512]{1,0:T(8,128)(2,1)S(1)}, bf16[512,512]{1,0:T(8,128)(2,1)}, u32[]{:S(2)}) copy-start(bf16[512,512]{1,0:T(8,128)(2,1)} %param.38) | copy-start | bytes 1572868
  7.2 47.6 %all-gather.2.cloned.1.call-start = ((), (), s32[]{:S(2)}) async-start(), calls=%async_computation.1 | async-start | bytes 1114112 | tf_op jit(solution)/shard_map/all_gather | solution.py:58
  7.9 235.5 %all-reduce.2.cloned.1.call-start = ((), (), s32[]{:S(2)}) async-start(), calls=%async_computation.2 | async-start | bytes 2097152 | tf_op jit(solution)/shard_map/psum | solution.py:98
  54.8 2.0 copy-start.11
  62.1 5.2 %copy-start.13 = (bf16[7,512]{1,0:T(8,128)(2,1)S(1)}, bf16[7,512]{1,0:T(8,128)(2,1)}, u32[]{:S(2)}) copy-start(bf16[7,512]{1,0:T(8,128)(2,1)} %get-tuple-element.309) | copy-start | bytes 21508 | tf_op jit(solution)/shard_map/while
  70.2 1.2 copy-start.2
  78.4 2.0 copy-start.11
  85.7 5.2 %copy-start.13 = (bf16[7,512]{1,0:T(8,128)(2,1)S(1)}, bf16[7,512]{1,0:T(8,128)(2,1)}, u32[]{:S(2)}) copy-start(bf16[7,512]{1,0:T(8,128)(2,1)} %get-tuple-element.309) | copy-start | bytes 21508 | tf_op jit(solution)/shard_map/while
  93.8 1.2 copy-start.2
  103.6 2.0 copy-start.11
  110.9 5.2 %copy-start.13 = (bf16[7,512]{1,0:T(8,128)(2,1)S(1)}, bf16[7,512]{1,0:T(8,128)(2,1)}, u32[]{:S(2)}) copy-start(bf16[7,512]{1,0:T(8,128)(2,1)} %get-tuple-element.309) | copy-start | bytes 21508 | tf_op jit(solution)/shard_map/while
  119.0 1.2 copy-start.2
  128.8 2.0 copy-start.11
  136.1 5.2 %copy-start.13 = (bf16[7,512]{1,0:T(8,128)(2,1)S(1)}, bf16[7,512]{1,0:T(8,128)(2,1)}, u32[]{:S(2)}) copy-start(bf16[7,512]{1,0:T(8,128)(2,1)} %get-tuple-element.309) | copy-start | bytes 21508 | tf_op jit(solution)/shard_map/while
  144.2 1.2 copy-start.2
  154.0 2.9 copy-start.10
  154.0 3.1 copy-start.3
  154.0 3.1 copy-start.4
  154.0 89.4 %copy-start.12 = (bf16[512,512]{1,0:T(8,128)(2,1)S(1)}, bf16[512,512]{1,0:T(8,128)(2,1)}, u32[]{:S(2)}) copy-start(bf16[512,512]{1,0:T(8,128)(2,1)} %param.32) | copy-start | bytes 1572868
  156.9 88.1 %copy-start.8 = (f32[512]{0:T(512)S(1)}, f32[512]{0:T(512)}, u32[]{:S(2)}) copy-start(f32[512]{0:T(512)} %param.33) | copy-start | bytes 6148
  157.4 97.9 %copy-start.7 = (s32[1024,3]{0,1:T(4,128)S(1)}, s32[1024,3]{0,1:T(4,128)}, u32[]{:S(2)}) copy-start(s32[1024,3]{0,1:T(4,128)} %param.36) | copy-start | bytes 36868
  245.1 12.7 %copy-start.5 = (bf16[64,512]{1,0:T(8,128)(2,1)}, bf16[64,512]{1,0:T(8,128)(2,1)S(1)}, u32[]{:S(2)}) copy-start(bf16[64,512]{1,0:T(8,128)(2,1)S(1)} %add_convert_fusion.2) | copy-start | bytes 196612
  246.4 22.7 %all-to-all-start = ((bf16[128,4,512]{2,1,0:T(4,128)(2,1)}), bf16[128,4,512]{2,1,0:T(4,128)(2,1)S(1)}, u32[]{:S(2)}, u32[]{:S(2)}) async-start(bf16[128,4,512]{2,1,0:T(4,128)(2,1)} %reshape.80), calls=%async_computation | async-start | bytes 1048576 | tf_op jit(solution)/shard_map/all_to_all | solution.py:112
  310.7 2.0 copy-start.9
  (8 other events, 8.9 us)
Sparse Core Ops, SparseCore 0:
  10.2 44.6 all-gather.1
  157.0 86.3 all-reduce.1
where the time goes:
time: 347 us; the launch traced here: 345 us
  waiting for transfers between devices  124 us (36%)
  matrix products  83.5 us (24%)
  local copies, waits for them, and re-layouts  66.4 us (19%)
  other arithmetic  31.3 us (9%)
  blocking collectives  15 us (4%)
  between operations  14.9 us (4%)
  starting transfers between devices  8.92 us (3%)
    psum x1, waiting for transfers between devices, on_device(): lax.psum(partial_value.astype(jnp.bfloat16), 'col').astype(jnp.float32)  86.1 us
    all_gather x1, waiting for transfers between devices, on_device(): receiver_block = lax.all_gather(nodes, 'col', axis=0, tiled=True)  26.4 us
    dot_general x10, matrix products, select_low(): jnp.dot(table_hot, table, preferred_element_type=jnp.float32)  22.4 us
    dot_general x4, matrix products, first_layer(): return jnp.dot(joined, joined_weight, preferred_element_type=jnp.float32)  20.7 us
    dot_general x6, matrix products, mlp_tail(): output = jnp.dot(hidden, second_weight, preferred_element_type=jnp.float32)  17.1 us
    dot_general x4, matrix products, edge_block(): lax.dot_general(recv_hot, kept, (((0,), (0,)), ((), ())), preferred_eleme...  16.6 us
    all_gather x1, blocking collectives, on_device(): sender_block = lax.all_gather(nodes, 'row', axis=0, tiled=True)  15 us
    all_to_all x1, waiting for transfers between devices, on_device(): lax.all_to_all(picked, ('row', 'col'), split_axis=0, concat_axis=0, tiled...  11.3 us
  transfers between devices with their start and end apart: 3, of which 3 were waited for; matrix products, arithmetic and copies ran while one was open for 2% of the time, Pallas kernels for 0%

commit v1 on v0

--- a/solution.py
+++ b/solution.py
@@ -95,7 +95,9 @@
         edge_block, jnp.zeros((receiver_count, width), jnp.float32), items
     )
     edges_out = edge_new.reshape(1, 1, capacity, width)
-    summed = lax.psum(partial_value.astype(jnp.bfloat16), "col").astype(jnp.float32)
+    summed = jnp.sum(lax.all_gather(partial_value.astype(jnp.bfloat16), "col"), axis=0).astype(
+        jnp.float32
+    )
     aggregated = lax.dynamic_slice_in_dim(summed, lax.axis_index("col") * node_block, node_block, 0)
     node_pre = jnp.dot(nodes, node_w1[0], preferred_element_type=jnp.float32)
     node_pre = node_pre + jnp.dot(

time: 347 us -> 392 us (1.13)
  waiting for transfers between devices: 124 us -> 150 us
  other arithmetic: 31.3 us -> 44.8 us
  matrix products: 83.5 us -> 90.1 us
    all_gather x0 -> x1, waiting for transfers between devices: none -> 112 us  [on_device(): lax.all_gather(partial_value.astype(jnp.bfloat16), 'col')]
    psum x1 -> x0, waiting for transfers between devices: 86.1 us -> none  [on_device(): lax.psum(partial_value.astype(jnp.bfloat16), 'col').astype(jnp.float32)]
    reduce_sum x0 -> x1, other arithmetic: none -> 8.92 us  [on_device(): jnp.sum(lax.all_gather(partial_value.astype(jnp.bfloat16), 'col'), axis=0)]
    dynamic_update_slice x8, local copies, waits for them, and re-layouts: 10.1 us -> 18.2 us  [on_device(): lax.scan(edge_block, jnp.zeros((receiver_count, width), jnp.float32), items)]
    while x40 -> x24, local copies, waits for them, and re-layouts: 7.65 us -> 0.06 us
    dot_general x10, matrix products: 22.4 us -> 27.3 us  [select_low(): jnp.dot(table_hot, table, preferred_element_type=jnp.float32)]
    broadcast_in_dim x5, other arithmetic: 6.03 us -> 10.7 us  [on_device(): lax.scan(edge_block, jnp.zeros((receiver_count, width), jnp.float32), items)]
where the time goes in v1:
time: 392 us; the launch traced here: 390 us
  waiting for transfers between devices  150 us (38%)
  matrix products  90.1 us (23%)
  local copies, waits for them, and re-layouts  66.8 us (17%)
  other arithmetic  44.8 us (11%)
  blocking collectives  15 us (4%)
  between operations  14.9 us (4%)
  starting transfers between devices  7.98 us (2%)
    all_gather x1, waiting for transfers between devices, on_device(): lax.all_gather(partial_value.astype(jnp.bfloat16), 'col')  112 us
    dot_general x10, matrix products, select_low(): jnp.dot(table_hot, table, preferred_element_type=jnp.float32)  27.3 us
    all_gather x1, waiting for transfers between devices, on_device(): receiver_block = lax.all_gather(nodes, 'col', axis=0, tiled=True)  26.4 us
    dot_general x4, matrix products, first_layer(): return jnp.dot(joined, joined_weight, preferred_element_type=jnp.float32)  22.4 us
    dynamic_update_slice x8, local copies, waits for them, and re-layouts, on_device(): lax.scan(edge_block, jnp.zeros((receiver_count, width), jnp.float32), items)  18.2 us
    dot_general x6, matrix products, mlp_tail(): output = jnp.dot(hidden, second_weight, preferred_element_type=jnp.float32)  17.4 us
    dot_general x4, matrix products, edge_block(): lax.dot_general(recv_hot, kept, (((0,), (0,)), ((), ())), preferred_eleme...  16.4 us
    all_gather x1, blocking collectives, on_device(): sender_block = lax.all_gather(nodes, 'row', axis=0, tiled=True)  15 us
  transfers between devices with their start and end apart: 3, of which 3 were waited for; matrix products, arithmetic and copies ran while one was open for 2% of the time, Pallas kernels for 0%

profile of v1, /device:TPU:1, one launch (start us, length us, event | category | flops | bytes accessed | tf_op | source)
XLA Modules:
  0.0 390.2 jit_solution(15681342501154550012)
XLA Ops:
  13.4 15.0 %all_gather.12 = bf16[512,512]{1,0:T(8,128)(2,1)S(1)} all-gather(bf16[64,512]{1,0:T(8,128)(2,1)} %param.21), channel_id=1, replica_groups=mesh['row'=8,'col'=16] {'row'}, dimensions={0}, use_global_device_ids=true | all-gather | bytes 589824 | tf_op jit(solution)/shard_map/all_gather | solution.py:57
  28.4 26.4 %all-gather.4.cloned.1.call-done = bf16[1024,512]{1,0:T(8,128)(2,1)} async-done(((bf16[64,512]{1,0:T(8,128)(2,1)}), bf16[1024,512]{1,0:T(8,128)(2,1)}) %all-gather.4.cloned.1.call-update) | async-done | bytes 1048592 | tf_op jit(solution)/shard_map/all_gather | solution.py:58
  54.8 110.7 %while.13 = (s32[]{:T(128)}, f32[1024,512]{1,0:T(8,128)}, bf16[4,1024,512]{2,1,0:T(8,128)(2,1)}, s32[4,1024]{1,0:T(4,128)S(1)}, pred[4,1024]{1,0:T(4,128)(4,1)S(...) while((s32[]{:T(128)}, f32[1024,512]{1,0:T(8,128)}, ...), condition=%wide.region_3.4_spmd.clone, body=%wide.region_0.3_spmd.clone.sunk | while | flops 4866973696 | bytes 40509184 | solution.py:94
  62.3 5.6 %fusion.97 = f32[1024,512]{1,0:T(8,128)} fusion(bf16[1536,512]{1,0:T(8,128)(2,1)} %get-tuple-element.307, bf16[1024,512]{0,1:T(8,128)(2,1)} %fusion.95, bf16[1024,512]{0,1:T(8,128)(2,1)} %fusion.96, bf16[1024,512]{0,1:T(8,128)(2,1)S(1)} %bitcast.65), kind=kOutput, calls=%fused_computation.3.clone.1 | convolution fusion | flops 1620049920 | bytes 6815744 | tf_op jit(solution)/shard_map/while/body/eval_jaxpr/dot_general | solution.py:65
  83.2 3.6 fusion.95
  88.8 5.6 %fusion.97 = f32[1024,512]{1,0:T(8,128)} fusion(bf16[1536,512]{1,0:T(8,128)(2,1)} %get-tuple-element.307, bf16[1024,512]{0,1:T(8,128)(2,1)} %fusion.95, bf16[1024,512]{0,1:T(8,128)(2,1)} %fusion.96, bf16[1024,512]{0,1:T(8,128)(2,1)S(1)} %bitcast.65), kind=kOutput, calls=%fused_computation.3.clone.1 | convolution fusion | flops 1620049920 | bytes 6815744 | tf_op jit(solution)/shard_map/while/body/eval_jaxpr/dot_general | solution.py:65
  104.9 4.5 %select_add_fusion.2 = f32[1024,512]{1,0:T(8,128)} fusion(f32[1024,512]{1,0:T(8,128)} %get-tuple-element.283, s32[1024]{0:T(1024)S(1)} %bitcast.69, pred[]{:T(512)S(6)} %compare.3, f32[1024,512]{0,1:T(8,128)S(1)} %get-tuple-element.264, f32[512]{0:T(512)S(1)} %copy-done.5, f32[1024]{0:T(1024)S(1)} %add_rsqrt_fusion.4, ...), kind=kOutput, calls=%fused_computation.10.clone.1 | convolution fusion | flops 1079508992 | bytes 6306817 | tf_op jit(solution)/shard_map/while/body/eval_jaxpr/dot_general | solution.py:89
  116.8 5.6 %fusion.97 = f32[1024,512]{1,0:T(8,128)} fusion(bf16[1536,512]{1,0:T(8,128)(2,1)} %get-tuple-element.307, bf16[1024,512]{0,1:T(8,128)(2,1)} %fusion.95, bf16[1024,512]{0,1:T(8,128)(2,1)} %fusion.96, bf16[1024,512]{0,1:T(8,128)(2,1)S(1)} %bitcast.65), kind=kOutput, calls=%fused_computation.3.clone.1 | convolution fusion | flops 1620049920 | bytes 6815744 | tf_op jit(solution)/shard_map/while/body/eval_jaxpr/dot_general | solution.py:65
  132.9 4.5 %select_add_fusion.2 = f32[1024,512]{1,0:T(8,128)} fusion(f32[1024,512]{1,0:T(8,128)} %get-tuple-element.283, s32[1024]{0:T(1024)S(1)} %bitcast.69, pred[]{:T(512)S(6)} %compare.3, f32[1024,512]{0,1:T(8,128)S(1)} %get-tuple-element.264, f32[512]{0:T(512)S(1)} %copy-done.5, f32[1024]{0:T(1024)S(1)} %add_rsqrt_fusion.4, ...), kind=kOutput, calls=%fused_computation.10.clone.1 | convolution fusion | flops 1079508992 | bytes 6306817 | tf_op jit(solution)/shard_map/while/body/eval_jaxpr/dot_general | solution.py:89
  144.9 5.6 %fusion.97 = f32[1024,512]{1,0:T(8,128)} fusion(bf16[1536,512]{1,0:T(8,128)(2,1)} %get-tuple-element.307, bf16[1024,512]{0,1:T(8,128)(2,1)} %fusion.95, bf16[1024,512]{0,1:T(8,128)(2,1)} %fusion.96, bf16[1024,512]{0,1:T(8,128)(2,1)S(1)} %bitcast.65), kind=kOutput, calls=%fused_computation.3.clone.1 | convolution fusion | flops 1620049920 | bytes 6815744 | tf_op jit(solution)/shard_map/while/body/eval_jaxpr/dot_general | solution.py:65
  161.0 4.5 %select_add_fusion.2 = f32[1024,512]{1,0:T(8,128)} fusion(f32[1024,512]{1,0:T(8,128)} %get-tuple-element.283, s32[1024]{0:T(1024)S(1)} %bitcast.69, pred[]{:T(512)S(6)} %compare.3, f32[1024,512]{0,1:T(8,128)S(1)} %get-tuple-element.264, f32[512]{0:T(512)S(1)} %copy-done.5, f32[1024]{0:T(1024)S(1)} %add_rsqrt_fusion.4, ...), kind=kOutput, calls=%fused_computation.10.clone.1 | convolution fusion | flops 1079508992 | bytes 6306817 | tf_op jit(solution)/shard_map/while/body/eval_jaxpr/dot_general | solution.py:89
  168.8 111.8 %all-gather.6.cloned.1.call-done = bf16[16384,512]{1,0:T(8,128)(2,1)} async-done(((bf16[1024,512]{1,0:T(8,128)(2,1)}), bf16[16384,512]{1,0:T(8,128)(2,1)}) %all-gather.6.cloned.1.call-update) | async-done | bytes 16777232 | tf_op jit(solution)/shard_map/all_gather | solution.py:98
  280.6 8.9 %reduce_sum.75 = bf16[1024,512]{1,0:T(8,128)(2,1)S(1)} reduce(bf16[16,1024,512]{2,1,0:T(8,128)(2,1)} %bitcast.66, bf16[]{:T(256)} %constant.53.clone.1), dimensions={0}, to_apply=%region_4.5 | reduce | flops 7864320 | bytes 17825794 | tf_op jit(solution)/shard_map/reduce_sum | solution.py:98
  292.7 7.9 %all-to-all-start = ((bf16[128,4,512]{2,1,0:T(4,128)(2,1)}), bf16[128,4,512]{2,1,0:T(4,128)(2,1)S(1)}, u32[]{:S(2)}, u32[]{:S(2)}) async-start(bf16[128,4,512]{2,1,0:T(4,128)(2,1)} %reshape.80), calls=%async_computation | async-start | bytes 1048576 | tf_op jit(solution)/shard_map/all_to_all | solution.py:114
  303.2 11.3 %all-to-all-done = bf16[128,4,512]{2,1,0:T(4,128)(2,1)S(1)} async-done(((bf16[128,4,512]{2,1,0:T(4,128)(2,1)}), bf16[128,4,512]{2,1,0:T(4,128)(2,1)S(1)}, u32[]{:S(2)}, u32[]{:S(2)}) %all-to-all-start) | async-done | bytes 524320 | tf_op jit(solution)/shard_map/all_to_all | solution.py:114
  315.4 4.7 %fusion.28 = bf16[3072,512]{1,0:T(8,128)(2,1)} fusion(bf16[512,512]{1,0:T(8,128)(2,1)} %reshape.81, s32[3072]{0:T(1024)S(1)} %eq.75), kind=kOutput, calls=%fused_computation.43 | convolution fusion | flops 1613758464 | bytes 3682304 | tf_op jit(solution)/shard_map/dot_general | solution.py:27
  320.1 9.1 %dot_general.50 = bf16[1024,3,512]{2,1,0:T(4,128)(2,1)} reshape(bf16[3072,512]{1,0:T(8,128)(2,1)} %fusion.28) | data formatting | bytes 6291456 | tf_op jit(solution)/shard_map/dot_general | solution.py:121
  329.2 4.4 %broadcast_add_fusion = f32[1024,3,512]{2,0,1:T(8,128)S(1)} fusion(f32[1024,512]{1,0:T(8,128)S(1)} %fusion.36, bf16[1024,3,512]{2,1,0:T(4,128)(2,1)} %dot_general.50, bf16[2,512,512]{2,1,0:T(8,128)(2,1)} %param.37), kind=kOutput, calls=%fused_computation.47 | convolution fusion | flops 1612185600 | bytes 13107200 | tf_op jit(solution)/shard_map/dot_general | solution.py:121
  333.6 7.5 %copy.29 = f32[1024,3,512]{2,1,0:T(4,128)} copy(f32[1024,3,512]{2,0,1:T(8,128)S(1)} %broadcast_add_fusion) | data formatting | bytes 12582912 | tf_op jit(solution)/shard_map/add | solution.py:125
  341.2 10.8 %reshape.82 = f32[3072,512]{1,0:T(8,128)} reshape(f32[1024,3,512]{2,1,0:T(4,128)} %copy.29) | data formatting | bytes 12582912 | tf_op jit(solution)/shard_map/reshape | solution.py:126
  351.9 4.2 %fusion.62 = (f32[3072]{0:T(1024)S(1)}, f32[3072,512]{1,0:T(8,128)S(1)}) fusion(bf16[512,512]{1,0:T(8,128)(2,1)S(1)} %copy-done, f32[3072,512]{1,0:T(8,128)} %reshape.82), kind=kOutput, calls=%fused_computation.81 | convolution fusion | flops 1620046848 | bytes 13119488 | tf_op jit(solution)/shard_map/dot_general | solution.py:18
  358.1 3.8 multiply_multiply_fusion
  361.9 10.5 %reshape.83 = f32[1024,3,512]{2,1,0:T(4,128)} reshape(f32[3072,512]{1,0:T(8,128)} %multiply_multiply_fusion) | data formatting | bytes 12582912 | tf_op jit(solution)/shard_map/reshape | solution.py:126
  372.4 8.4 %reduce_sum.80 = f32[1024,512]{1,0:T(8,128)S(1)} reduce(f32[1024,3,512]{2,1,0:T(4,128)} %reshape.83, f32[]{:T(128)} %constant.52.clone.1), dimensions={1}, to_apply=%region_9.10 | reduce | flops 1048576 | bytes 8388612 | tf_op jit(solution)/shard_map/reduce_sum | solution.py:129
  (129 shorter events, 90.8 us)
Async XLA Ops:
  7.2 344.7 %copy-start = (bf16[512,512]{1,0:T(8,128)(2,1)S(1)}, bf16[512,512]{1,0:T(8,128)(2,1)}, u32[]{:S(2)}) copy-start(bf16[512,512]{1,0:T(8,128)(2,1)} %param.38) | copy-start | bytes 1572868
  7.2 47.6 %all-gather.4.cloned.1.call-start = ((), (), s32[]{:S(2)}) async-start(), calls=%async_computation.1 | async-start | bytes 1114112 | tf_op jit(solution)/shard_map/all_gather | solution.py:58
  7.9 272.7 %all-gather.6.cloned.1.call-start = ((), (), s32[]{:S(2)}) async-start(), calls=%async_computation.2 | async-start | bytes 17825792 | tf_op jit(solution)/shard_map/all_gather | solution.py:98
  62.3 5.6 %copy-start.1 = (bf16[1,1024,512]{1,2,0:T(8,128)(2,1)}, bf16[1,1024,512]{1,2,0:T(8,128)(2,1)S(1)}, u32[]{:S(2)}) copy-start(bf16[1,1024,512]{1,2,0:T(8,128)(2,1)S(1)} %copy.40) | copy-start | bytes 3145732 | tf_op jit(solution)/shard_map/while
  62.3 5.6 %copy-start.10 = (bf16[7,512]{1,0:T(8,128)(2,1)S(1)}, bf16[7,512]{1,0:T(8,128)(2,1)}, u32[]{:S(2)}) copy-start(bf16[7,512]{1,0:T(8,128)(2,1)} %get-tuple-element.309) | copy-start | bytes 21508 | tf_op jit(solution)/shard_map/while
  67.9 3.3 copy-start.5
  88.7 5.6 %copy-start.1 = (bf16[1,1024,512]{1,2,0:T(8,128)(2,1)}, bf16[1,1024,512]{1,2,0:T(8,128)(2,1)S(1)}, u32[]{:S(2)}) copy-start(bf16[1,1024,512]{1,2,0:T(8,128)(2,1)S(1)} %copy.40) | copy-start | bytes 3145732 | tf_op jit(solution)/shard_map/while
  88.7 5.6 %copy-start.10 = (bf16[7,512]{1,0:T(8,128)(2,1)S(1)}, bf16[7,512]{1,0:T(8,128)(2,1)}, u32[]{:S(2)}) copy-start(bf16[7,512]{1,0:T(8,128)(2,1)} %get-tuple-element.309) | copy-start | bytes 21508 | tf_op jit(solution)/shard_map/while
  94.4 3.3 copy-start.5
  116.8 5.6 %copy-start.1 = (bf16[1,1024,512]{1,2,0:T(8,128)(2,1)}, bf16[1,1024,512]{1,2,0:T(8,128)(2,1)S(1)}, u32[]{:S(2)}) copy-start(bf16[1,1024,512]{1,2,0:T(8,128)(2,1)S(1)} %copy.40) | copy-start | bytes 3145732 | tf_op jit(solution)/shard_map/while
  116.8 5.6 %copy-start.10 = (bf16[7,512]{1,0:T(8,128)(2,1)S(1)}, bf16[7,512]{1,0:T(8,128)(2,1)}, u32[]{:S(2)}) copy-start(bf16[7,512]{1,0:T(8,128)(2,1)} %get-tuple-element.309) | copy-start | bytes 21508 | tf_op jit(solution)/shard_map/while
  122.4 3.3 copy-start.5
  144.9 5.6 %copy-start.1 = (bf16[1,1024,512]{1,2,0:T(8,128)(2,1)}, bf16[1,1024,512]{1,2,0:T(8,128)(2,1)S(1)}, u32[]{:S(2)}) copy-start(bf16[1,1024,512]{1,2,0:T(8,128)(2,1)S(1)} %copy.40) | copy-start | bytes 3145732 | tf_op jit(solution)/shard_map/while
  144.9 5.6 %copy-start.10 = (bf16[7,512]{1,0:T(8,128)(2,1)S(1)}, bf16[7,512]{1,0:T(8,128)(2,1)}, u32[]{:S(2)}) copy-start(bf16[7,512]{1,0:T(8,128)(2,1)} %get-tuple-element.309) | copy-start | bytes 21508 | tf_op jit(solution)/shard_map/while
  150.5 3.3 copy-start.5
  165.5 2.8 copy-start.9
  165.5 3.1 copy-start.2
  165.5 3.1 copy-start.3
  280.6 10.7 %copy-start.7 = (f32[512]{0:T(512)S(1)}, f32[512]{0:T(512)}, u32[]{:S(2)}) copy-start(f32[512]{0:T(512)} %param.33) | copy-start | bytes 6148
  289.5 11.1 %copy-start.6 = (s32[1024,3]{0,1:T(4,128)S(1)}, s32[1024,3]{0,1:T(4,128)}, u32[]{:S(2)}) copy-start(s32[1024,3]{0,1:T(4,128)} %param.36) | copy-start | bytes 36868
  291.4 11.8 %copy-start.4 = (bf16[64,512]{1,0:T(8,128)(2,1)}, bf16[64,512]{1,0:T(8,128)(2,1)S(1)}, u32[]{:S(2)}) copy-start(bf16[64,512]{1,0:T(8,128)(2,1)S(1)} %add_convert_fusion.2) | copy-start | bytes 196612
  292.7 21.8 %all-to-all-start = ((bf16[128,4,512]{2,1,0:T(4,128)(2,1)}), bf16[128,4,512]{2,1,0:T(4,128)(2,1)S(1)}, u32[]{:S(2)}, u32[]{:S(2)}) async-start(bf16[128,4,512]{2,1,0:T(4,128)(2,1)} %reshape.80), calls=%async_computation | async-start | bytes 1048576 | tf_op jit(solution)/shard_map/all_to_all | solution.py:114
  356.1 2.0 copy-start.8
Sparse Core Ops, SparseCore 0:
  10.2 44.6 all-gather.3
  168.4 112.1 all-gather.5
